TPU v7x, 32 devices: a whole 2x2x4 slice. The times are simulated.
32 devices in a mesh: sx: 2 (over y), sy: 4 (over z), af: 4 (over x, core).
Axes of the slice: x: 2, y: 2, z: 4, core: 2. Of those that a mesh axis runs over, the one named last changes fastest.
Arguments:
- sky_maps: float32 [64, 128, 1024], P('sx', 'sy', 'af'), may hold values from -16 to 25
- validity: int32 [64, 128], P('sx', 'sy'), may hold values 0 or 1
- row_taps: float32 [1024, 65], P('af'), may hold values from -0.75 to 0.75
- column_taps: float32 [1024, 65], P('af'), may hold values from -0.75 to 0.75
- init_loadings: float32 [1024, 32], P('af'), may hold values from -0.1875 to 0.1875
Outputs:
- cleaned_maps: float32 [64, 128, 1024], P('sx', 'sy', 'af')
- loadings: float32 [1024, 32], P('af')
- noise_var: float32 [], replicated
All inputs are finite; a program needn't handle non-finite values. No bound on the sum of `validity` on one device may be relied on, other than what follows from the above.
Results may differ from a plain program's by a relative error of at most 0.0003.
Values sent between devices are 32-bit elements; how exact they have to be, the bound alone decides.
A program may use at most 128 MiB of HBM per device.

v0:
```python
import math

import jax
import jax.numpy as jnp
from jax import lax
from jax.sharding import PartitionSpec as P

ITERS = 4


HIGHEST_PRECISION = lax.Precision.HIGHEST


def padded(block, sides, width):
    for axis, dim in sides:
        count = lax.axis_size(axis)
        forward = [(i, i + 1) for i in range(count - 1)]
        backward = [(target, source) for source, target in forward]
        low = lax.ppermute(
            lax.slice_in_dim(block, block.shape[dim] - width, None, axis=dim), axis, forward
        )
        high = lax.ppermute(lax.slice_in_dim(block, 0, width, axis=dim), axis, backward)
        block = jnp.concatenate([low, block, high], axis=dim)
    return block


def inverse_spd(matrix):
    identity = jnp.eye(matrix.shape[0], dtype=matrix.dtype)
    factor = jnp.linalg.cholesky(matrix)
    lower_inverse = lax.linalg.triangular_solve(factor, identity, left_side=True, lower=True)
    return jnp.dot(lower_inverse.T, lower_inverse, precision=HIGHEST_PRECISION)


def contract_rows(left_rows, right_rows):
    return lax.dot_general(
        left_rows, right_rows, (((0,), (0,)), ((), ())), precision=HIGHEST_PRECISION
    )


def correlate(extended, tap_table, out_length, along_dim):
    freq_count, tap_count = tap_table.shape
    block_size = math.gcd(freq_count, 32)
    in_length = extended.shape[along_dim]
    offsets = jnp.arange(in_length)[:, None] - jnp.arange(out_length)[None, :]
    one_hot = (offsets[None, :, :] == jnp.arange(tap_count)[:, None, None]).astype(jnp.float32)
    shape_out = list(extended.shape)
    shape_out[along_dim] = out_length
    filtered_all = jnp.zeros(tuple(shape_out), jnp.float32)

    def add_block(block_index, filtered_all):
        first_freq = block_index * block_size
        slab_part = lax.dynamic_slice_in_dim(extended, first_freq, block_size, 2)
        tap_block = lax.dynamic_slice_in_dim(tap_table, first_freq, block_size, 0)
        band_matrix = jnp.einsum("ft,tio->fio", tap_block, one_hot, precision=HIGHEST_PRECISION)
        if along_dim == 0:
            filtered = jnp.einsum(
                "icf,fio->ocf", slab_part, band_matrix, precision=HIGHEST_PRECISION
            )
        else:
            filtered = jnp.einsum(
                "rif,fio->rof", slab_part, band_matrix, precision=HIGHEST_PRECISION
            )
        return lax.dynamic_update_slice_in_dim(filtered_all, filtered, first_freq, 2)

    return lax.fori_loop(0, freq_count // block_size, add_block, filtered_all)


def latent_of(spectra, loadings, inverse):
    partial_latent = jnp.dot(
        spectra,
        jnp.dot(loadings, inverse, precision=HIGHEST_PRECISION),
        precision=HIGHEST_PRECISION,
    )
    return lax.psum(partial_latent, "af")


def gram_of(loadings, trace_local):
    return lax.psum((contract_rows(loadings, loadings), trace_local), "af")


def body(sky_maps, validity, row_taps, column_taps, init_loadings):
    rows_here, cols_here, freqs_here = sky_maps.shape
    halo_width = (row_taps.shape[1] - 1) // 2
    masked = sky_maps * validity.astype(jnp.float32)[:, :, None]
    extended = padded(masked, (("sx", 0), ("sy", 1)), halo_width)
    smoothed = correlate(extended, row_taps, rows_here, 0)
    beamed = correlate(smoothed, column_taps, cols_here, 1)
    spectra = beamed.reshape(rows_here * cols_here, freqs_here)
    total_power = lax.psum(jnp.sum(spectra * spectra), ("sx", "sy", "af"))
    pixel_count = rows_here * cols_here * lax.axis_size("sx") * lax.axis_size("sy")
    freq_total = freqs_here * lax.axis_size("af")
    components = init_loadings.shape[1]
    identity = jnp.eye(components, dtype=jnp.float32)
    noise_var = jnp.float32(1.0)
    loadings_block = init_loadings
    gram_matrix, unused_trace = gram_of(loadings_block, jnp.float32(0.0))
    for iteration in range(ITERS):
        inverse = inverse_spd(gram_matrix + noise_var * identity)
        latent = latent_of(spectra, loadings_block, inverse)
        cross_block, second = lax.psum(
            (contract_rows(spectra, latent), contract_rows(latent, latent)), ("sx", "sy")
        )
        scaled = pixel_count * noise_var * inverse + second
        updated = jnp.dot(cross_block, inverse_spd(scaled), precision=HIGHEST_PRECISION)
        gram_matrix, trace_total = gram_of(updated, jnp.sum(updated * cross_block))
        noise_var = (total_power - 2.0 * trace_total + jnp.sum(scaled * gram_matrix)) / (
            pixel_count * freq_total
        )
        loadings_block = updated
    inverse = inverse_spd(gram_matrix + noise_var * identity)
    latent = latent_of(spectra, loadings_block, inverse)
    cleaned = spectra - jnp.dot(latent, loadings_block.T, precision=HIGHEST_PRECISION)
    return (cleaned.reshape(rows_here, cols_here, freqs_here), loadings_block, noise_var)


def solution(mesh):
    placed = (P("sx", "sy", "af"), P("sx", "sy"), P("af", None), P("af", None), P("af", None))
    return jax.shard_map(
        body,
        mesh=mesh,
        in_specs=placed,
        out_specs=(P("sx", "sy", "af"), P("af", None), P()),
        check_vma=False,
    )
```

profile of v0, /device:TPU:0, one launch (start us, length us, event | category | flops | bytes accessed | tf_op | source)
XLA Modules:
  0.0 673.6 jit_solution(210484899642238842)
XLA Ops:
  9.4 4.9 collective-permute-start
  15.7 21.0 %collective-permute-done = f32[32,32,256]{2,1,0:T(8,128)S(1)} collective-permute-done((f32[32,32,256]{2,1,0:T(8,128)S(1)}, f32[32,32,256]{2,1,0:T(8,128)S(1)}, u32[]{:S(2)}, u32[]{:S(2)}) %collective-permute-start) | collective-permute-done | bytes 1048608 | tf_op jit(solution)/shard_map/ppermute | solution.py:19
  36.7 4.2 collective-permute-done.1
  40.9 2.0 pad_maximum_fusion.1
  42.9 5.2 collective-permute-start.2
  49.8 10.5 %psum.161 = f32[32,32]{0,1:T(8,128)S(1)} all-reduce(f32[32,32]{0,1:T(8,128)S(1)} %fusion.75), channel_id=1, replica_groups=mesh['sx'=2,'sy'=4,'af'=4] {'af'}, use_global_device_ids=true, to_apply=%region_4.0 | all-reduce | flops 1024 | bytes 8192 | tf_op jit(solution)/shard_map/psum | solution.py:78
  60.4 2.9 cholesky.149
  64.7 2.4 custom-call.13
  67.8 45.1 %collective-permute-done.2 = f32[96,32,256]{2,1,0:T(8,128)} collective-permute-done((f32[96,32,256]{2,1,0:T(8,128)}, f32[96,32,256]{2,1,0:T(8,128)}, u32[]{:S(2)}, u32[]{:S(2)}) %collective-permute-start.2) | collective-permute-done | bytes 3145760 | tf_op jit(solution)/shard_map/ppermute | solution.py:19
  112.9 5.8 collective-permute-done.3
  118.7 5.9 pad_maximum_fusion
  124.5 11.6 %copy.60 = f32[96,96,256]{1,0,2:T(8,128)} copy(f32[96,96,256]{2,1,0:T(8,128)} %pad_maximum_fusion) | data formatting | bytes 18874368
  136.2 2.5 broadcast_in_dim.5
  138.7 43.1 %while.28 = (s32[]{:T(128)}, f32[32,96,256]{1,0,2:T(8,128)}, f32[256,65]{1,0:T(8,128)S(1)}, f32[96,96,256]{1,0,2:T(8,128)}, s32[96,32]{0,1:T(8,128)S(1)}, /*index=5*/s32[]{:T(128)}, s32[]{:T(128)}, s32[]{:T(128)}, s32[]{:T(128)}) while((s32[]{:T(128)}, f32[32,96,256]{1,0,2:T(8,128)}, f32[256,65]{1,0:T(8,128)S(1)}, ...), condition=%wide.region_1.0_spmd.clone, body=%wide.region_0.0_spmd.clone.sunk | while | flops 190322688 | bytes 4777103 | solution.py:65
  140.1 4.0 fusion.200
  145.5 4.0 fusion.200
  150.9 3.9 fusion.200
  156.3 3.9 fusion.200
  161.7 3.9 fusion.200
  167.1 3.9 fusion.200
  172.5 3.9 fusion.200
  177.8 3.9 fusion.200
  181.8 2.5 broadcast_in_dim.4
  184.2 31.1 %while.29 = (s32[]{:T(128)}, f32[32,32,256]{0,1,2:T(8,128)}, f32[256,65]{1,0:T(8,128)S(1)}, f32[32,96,256]{1,0,2:T(8,128)}, s32[96,32]{0,1:T(8,128)S(1)}, /*index=5*/s32[]{:T(128)}, s32[]{:T(128)}, s32[]{:T(128)}, s32[]{:T(128)}) while((s32[]{:T(128)}, f32[32,32,256]{0,1,2:T(8,128)}, f32[256,65]{1,0:T(8,128)S(1)}, ...), condition=%wide.region_3.0_spmd.clone, body=%wide.region_2.0_spmd.clone.sunk | while | flops 114825224 | bytes 1868943 | solution.py:65
  185.0 3.1 fusion.206
  188.9 3.1 fusion.206
  192.8 3.1 fusion.206
  196.7 3.1 fusion.206
  200.6 3.1 fusion.206
  204.5 3.1 fusion.206
  208.4 3.1 fusion.206
  212.2 3.1 fusion.206
  215.3 4.1 copy.62
  221.2 3.9 multiply_reduce_fusion
  225.1 38.2 %psum.166 = f32[]{:T(128)} all-reduce(f32[]{:T(128)} %multiply_reduce_fusion), channel_id=1, replica_groups=mesh['sx'=2,'sy'=4,'af'=4] {'sx','sy','af'}, use_global_device_ids=true, to_apply=%region_12.15 | all-reduce | flops 1 | bytes 8 | tf_op jit(solution)/shard_map/psum | solution.py:89
  266.1 37.9 %all-reduce.3 = (f32[256,32]{0,1:T(8,128)S(1)}, f32[32,32]{0,1:T(8,128)S(1)}) all-reduce(f32[256,32]{0,1:T(8,128)S(1)} %fusion.79, f32[32,32]{0,1:T(8,128)S(1)} %fusion.80), channel_id=1, replica_groups=mesh['sx'=2,'sy'=4,'af'=4] {'sx','sy'}, use_global_device_ids=true, to_apply=%region_8.11 | all-reduce | flops 9216 | bytes 73728 | tf_op jit(solution)/shard_map/psum | solution.py:100
  304.1 2.9 cholesky.160
  308.4 2.4 custom-call.14
  312.3 11.3 %all-reduce.7 = (f32[32,32]{0,1:T(8,128)S(1)}, f32[]{:T(128)}) all-reduce(f32[32,32]{0,1:T(8,128)S(1)} %fusion.82, f32[]{:T(128)} %get-tuple-element.272), channel_id=1, replica_groups=mesh['sx'=2,'sy'=4,'af'=4] {'af'}, use_global_device_ids=true, to_apply=%region_10.13 | all-reduce | flops 1025 | bytes 8200 | tf_op jit(solution)/shard_map/psum | solution.py:78
  326.1 2.9 cholesky.171
  330.4 2.5 custom-call.15
  335.4 27.8 %all-reduce.16.cloned.1.call-done = f32[1024,32]{0,1:T(8,128)} async-done(((f32[1024,32]{0,1:T(8,128)}), f32[1024,32]{0,1:T(8,128)}) %all-reduce.16.cloned.1.call-update) | async-done | bytes 131088 | tf_op jit(solution)/shard_map/psum | solution.py:74
  366.0 37.9 %all-reduce.2 = (f32[256,32]{0,1:T(8,128)S(1)}, f32[32,32]{0,1:T(8,128)S(1)}) all-reduce(f32[256,32]{0,1:T(8,128)S(1)} %fusion.86, f32[32,32]{0,1:T(8,128)S(1)} %fusion.87), channel_id=1, replica_groups=mesh['sx'=2,'sy'=4,'af'=4] {'sx','sy'}, use_global_device_ids=true, to_apply=%region_17.20 | all-reduce | flops 9216 | bytes 73728 | tf_op jit(solution)/shard_map/psum | solution.py:100
  404.0 2.9 cholesky.182
  408.2 2.4 custom-call.16
  412.1 11.3 %all-reduce.6 = (f32[32,32]{0,1:T(8,128)S(1)}, f32[]{:T(128)}) all-reduce(f32[32,32]{0,1:T(8,128)S(1)} %fusion.89, f32[]{:T(128)} %get-tuple-element.274), channel_id=1, replica_groups=mesh['sx'=2,'sy'=4,'af'=4] {'af'}, use_global_device_ids=true, to_apply=%region_19.22 | all-reduce | flops 1025 | bytes 8200 | tf_op jit(solution)/shard_map/psum | solution.py:78
  426.0 2.9 cholesky.193
  430.2 2.5 custom-call.17
  435.2 27.9 %all-reduce.18.cloned.1.call-done = f32[1024,32]{0,1:T(8,128)} async-done(((f32[1024,32]{0,1:T(8,128)}), f32[1024,32]{0,1:T(8,128)}) %all-reduce.18.cloned.1.call-update) | async-done | bytes 131088 | tf_op jit(solution)/shard_map/psum | solution.py:74
  465.9 37.9 %all-reduce.1 = (f32[256,32]{0,1:T(8,128)S(1)}, f32[32,32]{0,1:T(8,128)S(1)}) all-reduce(f32[256,32]{0,1:T(8,128)S(1)} %fusion.93, f32[32,32]{0,1:T(8,128)S(1)} %fusion.94), channel_id=1, replica_groups=mesh['sx'=2,'sy'=4,'af'=4] {'sx','sy'}, use_global_device_ids=true, to_apply=%region_24.27 | all-reduce | flops 9216 | bytes 73728 | tf_op jit(solution)/shard_map/psum | solution.py:100
  503.9 2.9 cholesky.204
  508.1 2.4 custom-call.18
  512.0 11.5 %all-reduce.5 = (f32[32,32]{0,1:T(8,128)S(1)}, f32[]{:T(128)}) all-reduce(f32[32,32]{0,1:T(8,128)S(1)} %fusion.96, f32[]{:T(128)} %get-tuple-element.276), channel_id=1, replica_groups=mesh['sx'=2,'sy'=4,'af'=4] {'af'}, use_global_device_ids=true, to_apply=%region_26.29 | all-reduce | flops 1025 | bytes 8200 | tf_op jit(solution)/shard_map/psum | solution.py:78
  526.0 2.9 cholesky.215
  530.3 2.5 custom-call.19
  535.3 27.9 %all-reduce.20.cloned.1.call-done = f32[1024,32]{0,1:T(8,128)} async-done(((f32[1024,32]{0,1:T(8,128)}), f32[1024,32]{0,1:T(8,128)}) %all-reduce.20.cloned.1.call-update) | async-done | bytes 131088 | tf_op jit(solution)/shard_map/psum | solution.py:74
  565.9 37.9 %all-reduce = (f32[256,32]{0,1:T(8,128)S(1)}, f32[32,32]{0,1:T(8,128)S(1)}) all-reduce(f32[256,32]{0,1:T(8,128)S(1)} %fusion.100, f32[32,32]{0,1:T(8,128)S(1)} %fusion.101), channel_id=1, replica_groups=mesh['sx'=2,'sy'=4,'af'=4] {'sx','sy'}, use_global_device_ids=true, to_apply=%region_31.34 | all-reduce | flops 9216 | bytes 73728 | tf_op jit(solution)/shard_map/psum | solution.py:100
  603.9 2.9 cholesky.226
  608.2 2.4 custom-call.20
  612.1 11.3 %all-reduce.4 = (f32[32,32]{0,1:T(8,128)S(1)}, f32[]{:T(128)}) all-reduce(f32[32,32]{0,1:T(8,128)S(1)} %fusion.103, f32[]{:T(128)} %get-tuple-element.278), channel_id=1, replica_groups=mesh['sx'=2,'sy'=4,'af'=4] {'af'}, use_global_device_ids=true, to_apply=%region_33.36 | all-reduce | flops 1025 | bytes 8200 | tf_op jit(solution)/shard_map/psum | solution.py:78
  625.9 2.9 cholesky.237
  630.2 2.5 custom-call.21
  635.1 28.0 %all-reduce.22.cloned.1.call-done = f32[1024,32]{0,1:T(8,128)} async-done(((f32[1024,32]{0,1:T(8,128)}), f32[1024,32]{0,1:T(8,128)}) %all-reduce.22.cloned.1.call-update) | async-done | bytes 131088 | tf_op jit(solution)/shard_map/psum | solution.py:74
  663.0 2.9 convolution_subtract_fusion
  (157 shorter events, 67.4 us)
Async XLA Ops:
  7.2 42.4 %copy-start = (f32[256,32]{0,1:T(8,128)S(1)}, f32[256,32]{0,1:T(8,128)}, u32[]{:S(2)}) copy-start(f32[256,32]{0,1:T(8,128)} %param.16) | copy-start | bytes 98308
  7.2 256.1 %all-reduce.14.cloned.1.call-start = ((), (), s32[]{:S(2)}) async-start(), calls=%async_computation | async-start | bytes 262144 | tf_op jit(solution)/shard_map/psum | solution.py:74
  7.9 41.4 %copy-start.2 = (f32[256,65]{0,1:T(8,128)S(1)}, f32[256,65]{0,1:T(8,128)}, u32[]{:S(2)}) copy-start(f32[256,65]{0,1:T(8,128)} %param.14) | copy-start | bytes 199684
  7.9 41.6 %copy-start.3 = (f32[256,65]{0,1:T(8,128)S(1)}, f32[256,65]{0,1:T(8,128)}, u32[]{:S(2)}) copy-start(f32[256,65]{0,1:T(8,128)} %param.15) | copy-start | bytes 199684
  9.4 27.3 %collective-permute-start = (f32[32,32,256]{2,1,0:T(8,128)S(1)}, f32[32,32,256]{2,1,0:T(8,128)S(1)}, u32[]{:S(2)}, u32[]{:S(2)}) collective-permute-start(f32[32,32,256]{2,1,0:T(8,128)S(1)} %broadcast_multiply_fusion), channel_id=1, source_target_pairs={{0,16},{1,17},{2,18},{3,19},{4,20},{5,21},{6,22},{7,23},{8,24},{9,... | collective-permute-start | bytes 3145736 | tf_op jit(solution)/shard_map/ppermute | solution.py:19
  14.4 26.5 %collective-permute-start.1 = (f32[32,32,256]{2,1,0:T(8,128)S(1)}, f32[32,32,256]{2,1,0:T(8,128)S(1)}, u32[]{:S(2)}, u32[]{:S(2)}) collective-permute-start(f32[32,32,256]{2,1,0:T(8,128)S(1)} %broadcast_multiply_fusion), channel_id=1, source_target_pairs={{16,0},{17,1},{18,2},{19,3},{20,4},{21,5},{22,6},{23,7},{24,8},{25... | collective-permute-start | bytes 3145736 | tf_op jit(solution)/shard_map/ppermute | solution.py:22
  42.9 69.9 %collective-permute-start.2 = (f32[96,32,256]{2,1,0:T(8,128)}, f32[96,32,256]{2,1,0:T(8,128)}, u32[]{:S(2)}, u32[]{:S(2)}) collective-permute-start(f32[96,32,256]{2,1,0:T(8,128)} %pad_maximum_fusion.1), channel_id=1, source_target_pairs={{0,4},{4,8},{8,12},{1,5},{5,9},{9,13},{2,6},{6,10},{10,14},{3,7},{... | collective-permute-start | bytes 9437192 | tf_op jit(solution)/shard_map/ppermute | solution.py:19
  48.1 70.6 %collective-permute-start.3 = (f32[96,32,256]{2,1,0:T(8,128)}, f32[96,32,256]{2,1,0:T(8,128)}, u32[]{:S(2)}, u32[]{:S(2)}) collective-permute-start(f32[96,32,256]{2,1,0:T(8,128)} %pad_maximum_fusion.1), channel_id=1, source_target_pairs={{4,0},{8,4},{12,8},{5,1},{9,5},{13,9},{6,2},{10,6},{14,10},{7,3},{... | collective-permute-start | bytes 9437192 | tf_op jit(solution)/shard_map/ppermute | solution.py:22
  221.1 142.0 %all-reduce.16.cloned.1.call-start = ((), (), s32[]{:S(2)}) async-start(), calls=%async_computation.1 | async-start | bytes 262144 | tf_op jit(solution)/shard_map/psum | solution.py:74
  335.3 127.8 %all-reduce.18.cloned.1.call-start = ((), (), s32[]{:S(2)}) async-start(), calls=%async_computation.2 | async-start | bytes 262144 | tf_op jit(solution)/shard_map/psum | solution.py:74
  435.1 128.1 %all-reduce.20.cloned.1.call-start = ((), (), s32[]{:S(2)}) async-start(), calls=%async_computation.3 | async-start | bytes 262144 | tf_op jit(solution)/shard_map/psum | solution.py:74
  535.2 127.9 %all-reduce.22.cloned.1.call-start = ((), (), s32[]{:S(2)}) async-start(), calls=%async_computation.4 | async-start | bytes 262144 | tf_op jit(solution)/shard_map/psum | solution.py:74
  611.9 54.0 %copy-start.1 = (f32[256,32]{0,1:T(8,128)}, f32[256,32]{0,1:T(8,128)S(1)}, u32[]{:S(2)}) copy-start(f32[256,32]{0,1:T(8,128)S(1)} %get-tuple-element.279) | copy-start | bytes 98308
Sparse Core Ops, SparseCore 0:
  221.3 29.0 all-reduce.13
  335.4 27.7 all-reduce.15
  435.2 27.8 all-reduce.17
  535.3 27.8 all-reduce.19
  635.2 27.8 all-reduce.21
where the time goes:
time: 675 us; the launch traced here: 674 us
  blocking collectives  246 us (36%)
  waiting for transfers between devices  188 us (28%)
  matrix products  105 us (16%)
  other arithmetic  77.7 us (12%)
  between operations  22.8 us (3%)
  local copies, waits for them, and re-layouts  21.8 us (3%)
  starting transfers between devices  12.9 us (2%)
    psum x4, blocking collectives, body(): lax.psum((contract_rows(spectra, latent), contract_rows(latent, latent)),...  152 us
    psum x5, waiting for transfers between devices, latent_of(): return lax.psum(partial_latent, 'af')  112 us
    ppermute x2, waiting for transfers between devices, padded(): lax.ppermute(lax.slice_in_dim(block, block.shape[dim] - width, None, axis...  66.1 us
    psum x5, blocking collectives, gram_of(): return lax.psum((contract_rows(loadings, loadings), trace_local), 'af')  55.9 us
    psum x1, blocking collectives, body(): total_power = lax.psum(jnp.sum(spectra * spectra), ('sx', 'sy', 'af'))  38.2 us
    another operation x27, other arithmetic, inverse_spd(): factor = jnp.linalg.cholesky(matrix)  32.3 us
    dot_general x8, matrix products, add_block(): jnp.einsum('icf,fio->ocf', slab_part, band_matrix, precision=HIGHEST_PREC...  31.5 us
    another operation x18, other arithmetic, inverse_spd(): lax.linalg.triangular_solve(factor, identity, left_side=True, lower=True)  27.9 us
  transfers between devices with their start and end apart: 9, of which 8 were waited for; matrix products, arithmetic and copies ran while one was open for 2% of the time, Pallas kernels for 0%

commit v1 on v0

v1 whole, which is shorter than its diff:
```python
import functools

import jax
import jax.numpy as jnp
from jax import lax
from jax.experimental import pallas as pl
from jax.experimental.pallas import tpu as pltpu
from jax.sharding import PartitionSpec as P

ITERS = 4
EXACT = lax.Precision.HIGHEST
MESH = pl.DeviceIdType.MESH
F32 = jnp.float32


def dot_nn(left, right):
    return lax.dot_general(
        left, right, (((1,), (0,)), ((), ())), precision=EXACT, preferred_element_type=F32
    )


def dot_nt(left, right):
    return lax.dot_general(
        left, right, (((1,), (1,)), ((), ())), precision=EXACT, preferred_element_type=F32
    )


def inverse_spd(matrix):
    size = matrix.shape[0]
    sub = lax.broadcasted_iota(jnp.int32, (size, size), 0)
    lane = lax.broadcasted_iota(jnp.int32, (size, size), 1)
    for k in range(size):
        pivot = 1.0 / matrix[k : k + 1, k : k + 1]
        row = jnp.where(lane[:1] == k, pivot, matrix[k : k + 1, :] * pivot)
        col = matrix[:, k : k + 1]
        matrix = jnp.where(sub == k, row, jnp.where(lane == k, 0.0, matrix) - col * row)
    return matrix


def kernel(
    sizes, x_ref, rt_ref, ct_ref, l0_ref,
    out_ref, lout_ref, nv_ref,
    ext, cext, wr, wc, beamed, sp, lt, part, rsbuf, agbuf, mine, tpown, tpbuf, latg,
    y_send, y_recv, z_send, z_recv, l_send, l_recv, a_send, a_recv,
    tp_send, tp_recv, rs_send, rs_recv, ag_send, ag_recv, lat_send, lat_recv,
):
    nsx, nsy, naf = sizes
    ndev = nsx * nsy * naf
    rows, cols, freqs = x_ref.shape
    taps = rt_ref.shape[0]
    comps = l0_ref.shape[0]
    halo = (taps - 1) // 2
    fblocks = freqs // 128
    cgroups = cols // 8
    grows = rows // naf
    gpix = grows * cols
    pixels = rows * cols * nsx * nsy
    ftotal = freqs * naf
    tile_rows, tile_cols = comps // 8, ftotal // 128
    tiles = tile_rows * tile_cols

    sx, sy, af = lax.axis_index("sx"), lax.axis_index("sy"), lax.axis_index("af")
    me = (sx * nsy + sy) * naf + af

    def coords(flat):
        return (
            lax.div(flat, nsy * naf), lax.rem(lax.div(flat, naf), nsy), lax.rem(flat, naf)
        )

    barrier = pltpu.get_barrier_semaphore()

    def greet(k, carry):
        pl.semaphore_signal(
            barrier, inc=1, device_id=coords(lax.rem(me + k, ndev)), device_id_type=MESH
        )
        return carry

    lax.fori_loop(1, ndev, greet, 0)
    pl.semaphore_wait(barrier, ndev - 1)

    chunks = [(fb, cg) for fb in range(fblocks) for cg in range(cgroups)]

    def remote(src, dst, send, recv, target):
        return pltpu.make_async_remote_copy(
            src_ref=src, dst_ref=dst, send_sem=send, recv_sem=recv,
            device_id=target, device_id_type=MESH,
        )

    def y_copy(way, fb, cg):
        n = fb * cgroups + cg
        low = 0 if way == 0 else rows + halo
        return remote(
            x_ref.at[:, pl.ds(8 * cg, 8), pl.ds(128 * fb, 128)],
            ext.at[pl.ds(low, rows), pl.ds(8 * cg, 8), pl.ds(128 * fb, 128)],
            y_send.at[way, n], y_recv.at[way, n],
            (sx + 1 if way == 0 else sx - 1, sy, af),
        )

    def z_copy(way, fb, cg):
        n = fb * cgroups + cg
        low = 0 if way == 0 else cols + halo
        return remote(
            cext.at[:, pl.ds(halo + 8 * cg, 8), pl.ds(128 * fb, 128)],
            cext.at[:, pl.ds(low + 8 * cg, 8), pl.ds(128 * fb, 128)],
            z_send.at[way, n], z_recv.at[way, n],
            (sx, sy + 1 if way == 0 else sy - 1, af),
        )

    y_out = (sx < nsx - 1, sx > 0)
    y_in = (sx > 0, sx < nsx - 1)
    z_out = (sy < nsy - 1, sy > 0)
    z_in = (sy > 0, sy < nsy - 1)

    for way in range(2):
        @pl.when(y_out[way])
        def _():
            for fb, cg in chunks:
                y_copy(way, fb, cg).start()

    def l_copy(k):
        return remote(
            l0_ref, lt.at[af], l_send.at[k - 1], l_recv.at[k - 1],
            (sx, sy, lax.rem(af + k, naf)),
        )

    for k in range(1, naf):
        l_copy(k).start()
    lt[af] = l0_ref[...]

    for way in range(2):
        low = 0 if way == 0 else rows + halo

        @pl.when(jnp.logical_not(y_in[way]))
        def _():
            ext[pl.ds(low, halo)] = jnp.zeros((halo, cols, freqs), F32)

        @pl.when(jnp.logical_not(z_in[way]))
        def _():
            clow = 0 if way == 0 else cols + halo
            for r in range(rows):
                cext[r, pl.ds(clow, halo), :] = jnp.zeros((halo, freqs), F32)

    ext[pl.ds(halo, rows)] = x_ref[...]
    for t in range(taps):
        wr[t] = jnp.broadcast_to(rt_ref[pl.ds(t, 1), :], (8, freqs))
        wc[t] = jnp.broadcast_to(ct_ref[pl.ds(t, 1), :], (8, freqs))

    for fb, cg in chunks:
        n = fb * cgroups + cg
        for way in range(2):
            @pl.when(y_in[way])
            def _():
                y_copy(way, fb, cg).wait_recv()
        cs, fs = pl.ds(8 * cg, 8), pl.ds(128 * fb, 128)

        def add_tap(t, acc):
            return acc + wr[t, :, fs][None] * ext[pl.ds(t, rows), cs, fs]

        acc = lax.fori_loop(0, taps, add_tap, jnp.zeros((rows, 8, 128), F32))
        cext[:, pl.ds(halo + 8 * cg, 8), fs] = acc
        for way in range(2):
            @pl.when(z_out[way])
            def _():
                z_copy(way, fb, cg).start()

    def a_copy(k, fb):
        g = lax.rem(af + k, naf)
        return remote(
            beamed.at[pl.ds(g * gpix, gpix), pl.ds(128 * fb, 128)],
            sp.at[af, :, pl.ds(128 * fb, 128)],
            a_send.at[k - 1, fb], a_recv.at[k - 1, fb], (sx, sy, g),
        )

    power = jnp.zeros((8, 128), F32)
    for fb in range(fblocks):
        fs = pl.ds(128 * fb, 128)
        for way in range(2):
            @pl.when(z_in[way])
            def _():
                for cg in range(cgroups):
                    z_copy(way, fb, cg).wait_recv()
        for k in range(1, naf + 1):
            g = lax.rem(af + k, naf)

            def one_row(i, power):
                r = g * grows + i
                wide = cols // 8 + 1
                strip = cext[r, :, fs].reshape((cols + 2 * halo) // 8, 8, 128)
                total = jnp.zeros((cols, 128), F32)
                for s in range(8):
                    y = None
                    for t in range(s, taps, 8):
                        q = t // 8
                        if q + wide > strip.shape[0]:
                            last = strip[q : q + wide - 1] * wc[t, :, fs][None]
                            total = total + last.reshape(cols, 128)
                            continue
                        term = strip[q : q + wide] * wc[t, :, fs][None]
                        y = term if y is None else y + term
                    total = total + y.reshape(8 * wide, 128)[s : s + cols]
                beamed[pl.ds(pl.multiple_of(r * cols, 8), cols), fs] = total
                return power + jnp.sum((total * total).reshape(cols // 8, 8, 128), axis=0)

            power = lax.fori_loop(0, grows, one_row, power)
            if k < naf:
                a_copy(k, fb).start()
            else:
                sp[af, :, fs] = beamed[pl.ds(pl.multiple_of(af * gpix, 8), gpix), fs]

    def all_pairs(make):
        def step(k, carry):
            make(k).start()
            return carry
        lax.fori_loop(1, ndev, step, 0)

    tpown[...] = power
    tpbuf[me] = power
    all_pairs(lambda k: remote(
        tpown, tpbuf.at[me], tp_send, tp_recv, coords(lax.rem(me + k, ndev))
    ))
    for k in range(1, naf):
        l_copy(k).wait_recv()
        for fb in range(fblocks):
            a_copy(k, fb).wait_recv()

    def wide_of(ref):
        return jnp.concatenate([ref[a] for a in range(naf)], axis=1)

    eye = (
        lax.broadcasted_iota(jnp.int32, (comps, comps), 0)
        == lax.broadcasted_iota(jnp.int32, (comps, comps), 1)
    ).astype(F32)

    def latent_of(at):
        total = None
        for a in range(naf):
            term = dot_nt(at[:, freqs * a : freqs * (a + 1)], sp[a])
            total = term if total is None else total + term
        return total

    def pieces(ref, count):
        return ref.at[pl.ds(0, count)]

    def wait_all(ref, count, send, recv):
        return remote(pieces(ref, count), pieces(ref, count), send, recv, (sx, sy, af))

    wait_all(tpbuf, ndev - 1, tp_send, tp_recv).wait_recv()
    power = lax.fori_loop(1, ndev, lambda k, acc: acc + tpbuf[k], tpbuf[0])
    total_power = jnp.sum(jnp.sum(power, axis=1, keepdims=True), axis=0, keepdims=True)
    wait_all(tpbuf, ndev - 1, tp_send, tp_recv).wait_send()

    def total_of(value):
        return jnp.sum(jnp.sum(value, axis=1, keepdims=True), axis=0, keepdims=True)

    def em_step(iteration, carry):
        gram, noise = carry
        loadings = wide_of(lt)
        inverse = inverse_spd(gram + noise * eye)
        at = dot_nn(inverse, loadings)
        latent = latent_of(at)
        for a in range(naf):
            cross = dot_nn(latent, sp[a])
            for i in range(tile_rows):
                for j in range(freqs // 128):
                    part[i * tile_cols + a * (freqs // 128) + j] = cross[
                        8 * i : 8 * i + 8, 128 * j : 128 * j + 128
                    ]

        def scatter(k, carry):
            owner = lax.rem(me + k, ndev)

            @pl.when(owner < tiles)
            def _():
                remote(
                    part.at[owner], rsbuf.at[k - 1], rs_send, rs_recv, coords(owner)
                ).start()

            return carry

        lax.fori_loop(1, ndev, scatter, 0)

        @pl.when(me < tiles)
        def _():
            wait_all(rsbuf, ndev - 1, rs_send, rs_recv).wait_recv()
            full = lax.fori_loop(
                0, ndev - 1, lambda k, acc: acc + rsbuf[k], part[me], unroll=False
            )
            mine[...] = full
            agbuf[me] = full
            all_pairs(lambda k: remote(
                mine, agbuf.at[me], ag_send, ag_recv, coords(lax.rem(me + k, ndev))
            ))
            wait_all(agbuf, tiles - 1, ag_send, ag_recv).wait_recv()
            wait_all(part, tiles - 1, rs_send, rs_recv).wait_send()
            wait_all(rsbuf, ndev - 1, ag_send, ag_recv).wait_send()

        if ndev > tiles:
            @pl.when(me >= tiles)
            def _():
                wait_all(agbuf, tiles, ag_send, ag_recv).wait_recv()
                wait_all(part, tiles, rs_send, rs_recv).wait_send()

        cross = jnp.concatenate(
            [
                jnp.concatenate([agbuf[i * tile_cols + j] for j in range(tile_cols)], axis=1)
                for i in range(tile_rows)
            ],
            axis=0,
        )
        second = dot_nt(cross, at)
        scaled = (pixels * noise) * inverse + second
        updated = dot_nn(inverse_spd(scaled), cross)
        gram = dot_nt(updated, updated)
        trace = total_of(updated * cross)
        noise = (total_power - 2.0 * trace + total_of(scaled * gram)) / (pixels * ftotal)
        for a in range(naf):
            lt[a] = updated[:, freqs * a : freqs * (a + 1)]
        return gram, noise

    start = wide_of(lt)
    gram, noise = lax.fori_loop(
        0, ITERS, em_step, (dot_nt(start, start), jnp.ones((1, 1), F32))
    )
    nv_ref[...] = noise
    lout_ref[...] = lt[af]
    latent = latent_of(dot_nn(inverse_spd(gram + noise * eye), wide_of(lt)))
    latg[af] = latent

    def lat_copy(k):
        return remote(
            latg.at[af], latg.at[af], lat_send.at[k - 1], lat_recv.at[k - 1],
            (sx, sy, lax.rem(af + k, naf)),
        )

    for k in range(1, naf):
        lat_copy(k).start()
    for k in range(naf):
        if k > 0:
            lat_copy(k).wait_recv()
        g = lax.rem(af - k + naf, naf)
        span = pl.ds(pl.multiple_of(g * gpix, 8), gpix)
        out_ref[span, :] = beamed[span, :] - dot_nn(latg[g].T, lt[af])

    for way in range(2):
        @pl.when(y_out[way])
        def _():
            for fb, cg in chunks:
                y_copy(way, fb, cg).wait_send()

        @pl.when(z_out[way])
        def _():
            for fb, cg in chunks:
                z_copy(way, fb, cg).wait_send()
    for k in range(1, naf):
        l_copy(k).wait_send()
        lat_copy(k).wait_send()
        for fb in range(fblocks):
            a_copy(k, fb).wait_send()


def body(sizes, sky_maps, validity, row_taps, column_taps, init_loadings):
    rows, cols, freqs = sky_maps.shape
    comps = init_loadings.shape[1]
    taps = row_taps.shape[1]
    halo = (taps - 1) // 2
    nsx, nsy, naf = sizes
    ndev = nsx * nsy * naf
    tiles = (comps // 8) * (freqs * naf // 128)
    masked = sky_maps * validity.astype(F32)[:, :, None]
    vmem = pl.BlockSpec(memory_space=pltpu.VMEM)
    dma = pltpu.SemaphoreType.DMA
    count = (freqs // 128) * (cols // 8)
    cleaned, loadings, noise = pl.pallas_call(
        functools.partial(kernel, sizes),
        out_shape=(
            jax.ShapeDtypeStruct((rows * cols, freqs), F32),
            jax.ShapeDtypeStruct((comps, freqs), F32),
            jax.ShapeDtypeStruct((1, 1), F32),
        ),
        in_specs=[vmem] * 4,
        out_specs=(vmem, vmem, vmem),
        scratch_shapes=[
            pltpu.VMEM((rows + 2 * halo, cols, freqs), F32),
            pltpu.VMEM((rows, cols + 2 * halo, freqs), F32),
            pltpu.VMEM((taps, 8, freqs), F32),
            pltpu.VMEM((taps, 8, freqs), F32),
            pltpu.VMEM((rows * cols, freqs), F32),
            pltpu.VMEM((naf, rows * cols // naf, freqs), F32),
            pltpu.VMEM((naf, comps, freqs), F32),
            pltpu.VMEM((tiles, 8, 128), F32),
            pltpu.VMEM((ndev, 8, 128), F32),
            pltpu.VMEM((tiles, 8, 128), F32),
            pltpu.VMEM((8, 128), F32),
            pltpu.VMEM((8, 128), F32),
            pltpu.VMEM((ndev, 8, 128), F32),
            pltpu.VMEM((naf, comps, rows * cols // naf), F32),
            dma((2, count)), dma((2, count)), dma((2, count)), dma((2, count)),
            dma((naf - 1,)), dma((naf - 1,)),
            dma((naf - 1, freqs // 128)), dma((naf - 1, freqs // 128)),
            dma, dma, dma, dma, dma, dma,
            dma((naf - 1,)), dma((naf - 1,)),
        ],
        compiler_params=pltpu.CompilerParams(
            collective_id=0, has_side_effects=True, vmem_limit_bytes=48 * 1024 * 1024
        ),
        name="beam_pca",
    )(masked, row_taps.T, column_taps.T, init_loadings.T)
    return cleaned.reshape(rows, cols, freqs), loadings.T, noise[0, 0]


def solution(mesh):
    sizes = tuple(mesh.shape[axis] for axis in ("sx", "sy", "af"))
    placed = (P("sx", "sy", "af"), P("sx", "sy"), P("af", None), P("af", None), P("af", None))
    return jax.shard_map(
        functools.partial(body, sizes),
        mesh=mesh,
        in_specs=placed,
        out_specs=(P("sx", "sy", "af"), P("af", None), P()),
        check_vma=False,
    )
```

time: 675 us -> 146 us (0.22)
  blocking collectives: 246 us -> 0 us
  waiting for transfers between devices: 188 us -> 0 us
  Pallas kernels: 0 us -> 140 us
  matrix products: 105 us -> 0 us
  other arithmetic: 77.7 us -> 2.18 us
  between operations: 22.8 us -> 2.41 us
  local copies, waits for them, and re-layouts: 21.8 us -> 1.6 us
  starting transfers between devices: 12.9 us -> 0 us
    psum x10 -> x0, blocking collectives: 246 us -> none  [the longest x4 152 us: body(): lax.psum((contract_rows(spectra, latent), contract_rows(latent, latent)),...]
    pallas_call x0 -> x1, Pallas kernels: none -> 140 us  [body(): pl.pallas_call(functools.partial(kernel, sizes), out_shape=(jax.ShapeDtyp...]
    psum x5 -> x0, waiting for transfers between devices: 112 us -> none  [latent_of(): return lax.psum(partial_latent, 'af')]
    dot_general x69 -> x0, matrix products: 103 us -> none  [the longest x8 31.5 us: add_block(): jnp.einsum('icf,fio->ocf', slab_part, band_matrix, precision=HIGHEST_PREC...]
    ppermute x4 -> x0, waiting for transfers between devices: 76.1 us -> none  [the longest x2 66.1 us: padded(): lax.ppermute(lax.slice_in_dim(block, block.shape[dim] - width, None, axis...]
    another operation x45 -> x0, other arithmetic: 60.2 us -> none  [the longest x27 32.3 us: inverse_spd(): factor = jnp.linalg.cholesky(matrix)]
    ppermute x4 -> x0, starting transfers between devices: 12.7 us -> none  [the longest x2 10.1 us: padded(): lax.ppermute(lax.slice_in_dim(block, block.shape[dim] - width, None, axis...]
    unnamed x11 -> x8, local copies, waits for them, and re-layouts: 11.9 us -> 1.6 us
  transfers between devices with their start and end apart: 9 -> 0, of which waited for: 8 -> 0; matrix products, arithmetic and copies ran while one was open for 2% -> 0% of each run, Pallas kernels for 0% -> 0%
where the time goes in v1:
time: 146 us
  Pallas kernels  140 us (96%)
  between operations  2.41 us (2%)
  other arithmetic  2.18 us (1%)
  local copies, waits for them, and re-layouts  1.6 us (1%)
    pallas_call x1, Pallas kernels, body(): pl.pallas_call(functools.partial(kernel, sizes), out_shape=(jax.ShapeDtyp...  140 us

profile of v1, /device:TPU:0, one launch (start us, length us, event | category | flops | bytes accessed | tf_op | source)
XLA Modules:
  0.0 145.9 jit_solution(12113856833121329608)
XLA Ops:
  0.6 0.7 convert_element_type.3
  1.4 0.0 copy-start
  1.4 0.0 copy-start.1
  1.4 0.0 copy-start.2
  1.4 1.5 %broadcast_multiply_fusion.x_ref = f32[32,32,256]{2,1,0:T(8,128)S(1)} fusion(f32[32,32,256]{2,1,0:T(8,128)} %param.5, f32[32,32]{1,0:T(8,128)S(1)} %convert_element_type.3), kind=kLoop, calls=%fused_computation | loop fusion | flops 262144 | bytes 2101248 | tf_op jit(solution)/shard_map/mul | solution.py:369
  2.8 0.0 copy-done
  2.8 0.0 copy-done.1
  2.8 0.0 copy-done.2
  2.9 139.7 %beam_pca.1 = (f32[1024,256]{1,0:T(8,128)S(1)}, f32[32,256]{1,0:T(8,128)S(1)}, f32[1,1]{1,0:T(1,128)}) custom-call(f32[32,32,256]{2,1,0:T(8,128)S(1)} %broadcast_multiply_fusion.x_ref, f32[65,256]{1,0:T(8,128)S(1)} %bitcast.7, f32[65,256]{1,0:T(8,128)S(1)} %bitcast.8, f32[32,256]{1,0:T(8,128)S(1)} %bitcast.9), custom_call_target="tpu_custom_call" | custom-call | tf_op jit(solution)/shard_map/beam_pca/pallas_call | solution.py:373
  142.5 1.0 copy.11
  143.5 0.6 copy.12
Async XLA Ops:
  1.4 1.5 %copy-start = (f32[256,65]{0,1:T(8,128)S(1)}, f32[256,65]{0,1:T(8,128)}, u32[]{:S(2)}) copy-start(f32[256,65]{0,1:T(8,128)} %param.7) | copy-start | bytes 199684
  1.4 1.5 %copy-start.1 = (f32[256,65]{0,1:T(8,128)S(1)}, f32[256,65]{0,1:T(8,128)}, u32[]{:S(2)}) copy-start(f32[256,65]{0,1:T(8,128)} %param.8) | copy-start | bytes 199684
  1.4 1.5 %copy-start.2 = (f32[256,32]{0,1:T(8,128)S(1)}, f32[256,32]{0,1:T(8,128)}, u32[]{:S(2)}) copy-start(f32[256,32]{0,1:T(8,128)} %param.9) | copy-start | bytes 98308

commit v2 on v1

--- a/solution.py
+++ b/solution.py
@@ -26,21 +26,47 @@
 
 
 def inverse_spd(matrix):
-    size = matrix.shape[0]
+    size, step = matrix.shape[0], 4
     sub = lax.broadcasted_iota(jnp.int32, (size, size), 0)
     lane = lax.broadcasted_iota(jnp.int32, (size, size), 1)
-    for k in range(size):
-        pivot = 1.0 / matrix[k : k + 1, k : k + 1]
-        row = jnp.where(lane[:1] == k, pivot, matrix[k : k + 1, :] * pivot)
-        col = matrix[:, k : k + 1]
-        matrix = jnp.where(sub == k, row, jnp.where(lane == k, 0.0, matrix) - col * row)
+    lane8 = lane[:8]
+    for k in range(0, size, step):
+        span = range(step)
+        rows = [jnp.broadcast_to(matrix[k + i : k + i + 1, :], (8, size)) for i in span]
+        cols = [jnp.broadcast_to(matrix[:, k + j : k + j + 1], (size, size)) for j in span]
+        small = [
+            [jnp.broadcast_to(cols[j][k + i : k + i + 1, :], (8, size)) for j in span]
+            for i in span
+        ]
+        for m in span:
+            pivot = 1.0 / small[m][m]
+            line = [pivot if j == m else small[m][j] * pivot for j in span]
+            small = [
+                line if i == m else [
+                    (0.0 if j == m else small[i][j]) - small[i][m] * line[j] for j in span
+                ]
+                for i in span
+            ]
+        inside = jnp.logical_and(lane >= k, lane < k + step)
+        fresh = jnp.where(inside, 0.0, matrix)
+        lines = []
+        for i in span:
+            line = sum(small[i][j] * rows[j] for j in span)
+            for j in span:
+                line = jnp.where(lane8 == k + j, small[i][j], line)
+            line = jnp.concatenate([line] * (size // 8), axis=0)
+            fresh = fresh - cols[i] * line
+            lines.append(line)
+        for i in span:
+            fresh = jnp.where(sub == k + i, lines[i], fresh)
+        matrix = fresh
     return matrix
 
 
 def kernel(
     sizes, x_ref, rt_ref, ct_ref, l0_ref,
     out_ref, lout_ref, nv_ref,
-    ext, cext, wr, wc, beamed, sp, lt, part, rsbuf, agbuf, mine, tpown, tpbuf, latg,
+    ext, cext, wr, wc, beamed, sp, lt, part, rsbuf, agbuf, mine, tpown, tpbuf, latg, crossbuf,
     y_send, y_recv, z_send, z_recv, l_send, l_recv, a_send, a_recv,
     tp_send, tp_recv, rs_send, rs_recv, ag_send, ag_recv, lat_send, lat_recv,
 ):
@@ -62,20 +88,17 @@
     sx, sy, af = lax.axis_index("sx"), lax.axis_index("sy"), lax.axis_index("af")
     me = (sx * nsy + sy) * naf + af
 
-    def coords(flat):
-        return (
-            lax.div(flat, nsy * naf), lax.rem(lax.div(flat, naf), nsy), lax.rem(flat, naf)
-        )
+    sx_at = [lax.rem(sx + i, nsx) for i in range(nsx)]
+    sy_at = [lax.rem(sy + i, nsy) for i in range(nsy)]
+    af_at = [lax.rem(af + i, naf) for i in range(naf)]
+    peers = [
+        (x, y, z) for x in sx_at for y in sy_at for z in af_at
+    ][1:]
 
     barrier = pltpu.get_barrier_semaphore()
 
-    def greet(k, carry):
-        pl.semaphore_signal(
-            barrier, inc=1, device_id=coords(lax.rem(me + k, ndev)), device_id_type=MESH
-        )
-        return carry
-
-    lax.fori_loop(1, ndev, greet, 0)
+    for peer in peers:
+        pl.semaphore_signal(barrier, inc=1, device_id=peer, device_id_type=MESH)
     pl.semaphore_wait(barrier, ndev - 1)
 
     chunks = [(fb, cg) for fb in range(fblocks) for cg in range(cgroups)]
@@ -207,17 +230,14 @@
             else:
                 sp[af, :, fs] = beamed[pl.ds(pl.multiple_of(af * gpix, 8), gpix), fs]
 
-    def all_pairs(make):
-        def step(k, carry):
-            make(k).start()
-            return carry
-        lax.fori_loop(1, ndev, step, 0)
+    def all_pairs(src, dst, send, recv):
+        for peer in peers:
+            remote(src, dst, send, recv, peer).start()
 
     tpown[...] = power
     tpbuf[me] = power
-    all_pairs(lambda k: remote(
-        tpown, tpbuf.at[me], tp_send, tp_recv, coords(lax.rem(me + k, ndev))
-    ))
+    all_pairs(tpown, tpbuf.at[me], tp_send, tp_recv)
+    crossbuf[...] = jnp.zeros((comps, ftotal), F32)
     for k in range(1, naf):
         l_copy(k).wait_recv()
         for fb in range(fblocks):
@@ -252,12 +272,26 @@
     def total_of(value):
         return jnp.sum(jnp.sum(value, axis=1, keepdims=True), axis=0, keepdims=True)
 
+    def noise_of():
+        fitted = total_of(wide_of(lt) * crossbuf[...])
+        return (total_power - fitted) / (pixels * ftotal)
+
+    def gather():
+        wait_all(rsbuf, ndev - 1, rs_send, rs_recv).wait_recv()
+        full = part[me]
+        for k in range(min(ndev, 32) - 1):
+            full = full + rsbuf[k]
+        if ndev > 32:
+            full = lax.fori_loop(31, ndev - 1, lambda k, acc: acc + rsbuf[k], full)
+        mine[...] = full
+        agbuf[me] = full
+        all_pairs(mine, agbuf.at[me], ag_send, ag_recv)
+        wait_all(agbuf, tiles - 1, ag_send, ag_recv).wait_recv()
+        wait_all(part, tiles - 1, rs_send, rs_recv).wait_send()
+        wait_all(rsbuf, ndev - 1, ag_send, ag_recv).wait_send()
+
     def em_step(iteration, carry):
-        gram, noise = carry
-        loadings = wide_of(lt)
-        inverse = inverse_spd(gram + noise * eye)
-        at = dot_nn(inverse, loadings)
-        latent = latent_of(at)
+        latent = latent_of(wide_of(lt))
         for a in range(naf):
             cross = dot_nn(latent, sp[a])
             for i in range(tile_rows):
@@ -265,66 +299,46 @@
                     part[i * tile_cols + a * (freqs // 128) + j] = cross[
                         8 * i : 8 * i + 8, 128 * j : 128 * j + 128
                     ]
-
-        def scatter(k, carry):
-            owner = lax.rem(me + k, ndev)
-
-            @pl.when(owner < tiles)
-            def _():
-                remote(
-                    part.at[owner], rsbuf.at[k - 1], rs_send, rs_recv, coords(owner)
-                ).start()
-
-            return carry
-
-        lax.fori_loop(1, ndev, scatter, 0)
-
-        @pl.when(me < tiles)
-        def _():
-            wait_all(rsbuf, ndev - 1, rs_send, rs_recv).wait_recv()
-            full = lax.fori_loop(
-                0, ndev - 1, lambda k, acc: acc + rsbuf[k], part[me], unroll=False
-            )
-            mine[...] = full
-            agbuf[me] = full
-            all_pairs(lambda k: remote(
-                mine, agbuf.at[me], ag_send, ag_recv, coords(lax.rem(me + k, ndev))
-            ))
-            wait_all(agbuf, tiles - 1, ag_send, ag_recv).wait_recv()
-            wait_all(part, tiles - 1, rs_send, rs_recv).wait_send()
-            wait_all(rsbuf, ndev - 1, ag_send, ag_recv).wait_send()
+        for k, peer in enumerate(peers):
+            owner = (peer[0] * nsy + peer[1]) * naf + peer[2]
+            copy = (lambda: remote(part.at[owner], rsbuf.at[k], rs_send, rs_recv, peer).start())
+            if ndev > tiles:
+                pl.when(owner < tiles)(copy)
+            else:
+                copy()
+
+        loadings = wide_of(lt)
+        noise = jnp.where(iteration == 0, jnp.ones((1, 1), F32), noise_of())
+        inverse = inverse_spd(dot_nt(loadings, loadings) + noise * eye)
+        at = dot_nn(inverse, loadings)
 
         if ndev > tiles:
+            pl.when(me < tiles)(gather)
+
             @pl.when(me >= tiles)
             def _():
                 wait_all(agbuf, tiles, ag_send, ag_recv).wait_recv()
                 wait_all(part, tiles, rs_send, rs_recv).wait_send()
-
-        cross = jnp.concatenate(
+        else:
+            gather()
+
+        moment = jnp.concatenate(
             [
                 jnp.concatenate([agbuf[i * tile_cols + j] for j in range(tile_cols)], axis=1)
                 for i in range(tile_rows)
             ],
             axis=0,
         )
-        second = dot_nt(cross, at)
-        scaled = (pixels * noise) * inverse + second
+        cross = dot_nn(inverse, moment)
+        scaled = (pixels * noise) * inverse + dot_nt(cross, at)
         updated = dot_nn(inverse_spd(scaled), cross)
-        gram = dot_nt(updated, updated)
-        trace = total_of(updated * cross)
-        noise = (total_power - 2.0 * trace + total_of(scaled * gram)) / (pixels * ftotal)
+        crossbuf[...] = cross
         for a in range(naf):
             lt[a] = updated[:, freqs * a : freqs * (a + 1)]
-        return gram, noise
-
-    start = wide_of(lt)
-    gram, noise = lax.fori_loop(
-        0, ITERS, em_step, (dot_nt(start, start), jnp.ones((1, 1), F32))
-    )
-    nv_ref[...] = noise
-    lout_ref[...] = lt[af]
-    latent = latent_of(dot_nn(inverse_spd(gram + noise * eye), wide_of(lt)))
-    latg[af] = latent
+        return carry
+
+    lax.fori_loop(0, ITERS, em_step, 0)
+    latg[af] = latent_of(wide_of(lt))
 
     def lat_copy(k):
         return remote(
@@ -334,12 +348,18 @@
 
     for k in range(1, naf):
         lat_copy(k).start()
+    loadings = wide_of(lt)
+    noise = noise_of()
+    nv_ref[...] = noise
+    lout_ref[...] = lt[af]
+    inverse = inverse_spd(dot_nt(loadings, loadings) + noise * eye)
+    at_here = dot_nn(inverse, lt[af])
     for k in range(naf):
         if k > 0:
             lat_copy(k).wait_recv()
         g = lax.rem(af - k + naf, naf)
         span = pl.ds(pl.multiple_of(g * gpix, 8), gpix)
-        out_ref[span, :] = beamed[span, :] - dot_nn(latg[g].T, lt[af])
+        out_ref[span, :] = beamed[span, :] - dot_nn(latg[g].T, at_here)
 
     for way in range(2):
         @pl.when(y_out[way])
@@ -394,6 +414,7 @@
             pltpu.VMEM((8, 128), F32),
             pltpu.VMEM((ndev, 8, 128), F32),
             pltpu.VMEM((naf, comps, rows * cols // naf), F32),
+            pltpu.VMEM((comps, freqs * naf), F32),
             dma((2, count)), dma((2, count)), dma((2, count)), dma((2, count)),
             dma((naf - 1,)), dma((naf - 1,)),
             dma((naf - 1, freqs // 128)), dma((naf - 1, freqs // 128)),

time: 146 us -> 128 us (0.88)
  Pallas kernels: 140 us -> 121 us
    pallas_call x1, Pallas kernels: 140 us -> 121 us  [body(): pl.pallas_call(functools.partial(kernel, sizes), out_shape=(jax.ShapeDtyp...]
where the time goes in v2:
time: 128 us
  Pallas kernels  121 us (95%)
  between operations  2.41 us (2%)
  other arithmetic  2.18 us (2%)
  local copies, waits for them, and re-layouts  1.6 us (1%)
    pallas_call x1, Pallas kernels, body(): pl.pallas_call(functools.partial(kernel, sizes), out_shape=(jax.ShapeDtyp...  121 us

profile of v2, /device:TPU:0, one launch (start us, length us, event | category | flops | bytes accessed | tf_op | source)
XLA Modules:
  0.0 127.6 jit_solution(5600274365562875675)
XLA Ops:
  0.6 0.7 convert_element_type.3
  1.4 0.0 copy-start
  1.4 0.0 copy-start.1
  1.4 0.0 copy-start.2
  1.4 1.5 %broadcast_multiply_fusion.x_ref = f32[32,32,256]{2,1,0:T(8,128)S(1)} fusion(f32[32,32,256]{2,1,0:T(8,128)} %param.5, f32[32,32]{1,0:T(8,128)S(1)} %convert_element_type.3), kind=kLoop, calls=%fused_computation | loop fusion | flops 262144 | bytes 2101248 | tf_op jit(solution)/shard_map/mul | solution.py:389
  2.8 0.0 copy-done
  2.8 0.0 copy-done.1
  2.8 0.0 copy-done.2
  2.9 121.4 %beam_pca.1 = (f32[1024,256]{1,0:T(8,128)S(1)}, f32[32,256]{1,0:T(8,128)S(1)}, f32[1,1]{1,0:T(1,128)}) custom-call(f32[32,32,256]{2,1,0:T(8,128)S(1)} %broadcast_multiply_fusion.x_ref, f32[65,256]{1,0:T(8,128)S(1)} %bitcast.7, f32[65,256]{1,0:T(8,128)S(1)} %bitcast.8, f32[32,256]{1,0:T(8,128)S(1)} %bitcast.9), custom_call_target="tpu_custom_call" | custom-call | tf_op jit(solution)/shard_map/beam_pca/pallas_call | solution.py:393
  124.3 1.0 copy.11
  125.2 0.6 copy.12
Async XLA Ops:
  1.4 1.5 %copy-start = (f32[256,65]{0,1:T(8,128)S(1)}, f32[256,65]{0,1:T(8,128)}, u32[]{:S(2)}) copy-start(f32[256,65]{0,1:T(8,128)} %param.7) | copy-start | bytes 199684
  1.4 1.5 %copy-start.1 = (f32[256,65]{0,1:T(8,128)S(1)}, f32[256,65]{0,1:T(8,128)}, u32[]{:S(2)}) copy-start(f32[256,65]{0,1:T(8,128)} %param.8) | copy-start | bytes 199684
  1.4 1.5 %copy-start.2 = (f32[256,32]{0,1:T(8,128)S(1)}, f32[256,32]{0,1:T(8,128)}, u32[]{:S(2)}) copy-start(f32[256,32]{0,1:T(8,128)} %param.9) | copy-start | bytes 98308
